TPU v7x, 256 devices: a whole 4x4x8 slice. The times are simulated.
256 devices in a mesh: row: 16 (over y, z_hi, core), col: 16 (over x, z_lo).
Axes of the slice: x: 4, y: 4, z: 8 (z_hi: 2, z_lo: 4; z = z_hi * 4 + z_lo), core: 2. Of those that a mesh axis runs over, the one named last changes fastest.
Arguments:
- activations: bfloat16 [2048, 12800], P('row', 'col'), may hold values from -6 to 6
- task_weight: float32 [16], replicated, may hold values from 0.0625 to 0.25
Outputs:
- trailing: float32 [12800, 12800], P('row', 'col')
- panels: float32 [12800, 512], P('row', 'col')
All inputs are finite; a program needn't handle non-finite values.
Results may differ from a plain program's by a relative error of at most 0.0042.
Values may be sent and summed in bfloat16 or wider, within the bound.
A program may use at most 64 MiB of HBM per device.

v0:
```python
import jax
import jax.numpy as jnp
from jax import lax
from jax.sharding import PartitionSpec as P

TASKS = 16
TOK = 128
PANEL = 256


alpha_scale = 0.9
ridge_value = 0.2


def broadcast(shard, axis, root):
    mine = lax.axis_index(axis) == root
    return lax.psum(jnp.where(mine, shard, jnp.zeros_like(shard)), axis)


def factor_panel(panel_strip, diag_block, offset, first_row):
    factor_lower = jnp.linalg.cholesky(diag_block)
    width = diag_block.shape[0]
    solved = jax.scipy.linalg.solve_triangular(factor_lower, panel_strip.T, lower=True).T
    patched = jnp.concatenate(
        [jnp.zeros((offset, width), jnp.float32), factor_lower, solved[offset + width :]], 0
    )
    return jnp.where(first_row, patched, solved)


def outer_update(matrix_tile, left_rows, right_rows):
    return matrix_tile - jnp.dot(left_rows, right_rows.T, precision=lax.Precision.HIGHEST)


def body(activations, task_weight):
    row_count = lax.axis_size("row")
    col_count = lax.axis_size("col")
    my_row = lax.axis_index("row")
    my_col = lax.axis_index("col")
    per_owner = col_count // row_count
    tasks_local = TASKS // row_count
    local_cols = activations.shape[1]
    local_rows = local_cols * col_count // row_count
    width = PANEL
    own_weight = lax.dynamic_slice_in_dim(task_weight, my_row * tasks_local, tasks_local)
    factor = jnp.repeat(jnp.sqrt(own_weight / TOK), TOK)
    scaled = (activations.astype(jnp.float32) * factor[:, None]).astype(jnp.bfloat16)
    col_slab = lax.all_gather(scaled, "row", axis=0, tiled=True)
    owned = broadcast(col_slab, "col", my_row * per_owner + 0)
    gram_tile = lax.dot_general(
        owned, col_slab, (((0,), (0,)), ((), ())), preferred_element_type=jnp.float32
    )
    global_row = my_row * local_rows + jnp.arange(local_rows)[:, None]
    global_col = my_col * local_cols + jnp.arange(local_cols)[None, :]
    matrix_tile = jnp.where(
        global_row == global_col, gram_tile + ridge_value, alpha_scale * gram_tile
    )
    first_row = my_row == 0
    gathered_rows = []
    for panel_index in range(2):
        offset = panel_index * width
        diag_block = broadcast(
            matrix_tile[offset : offset + width, offset : offset + width], "row", 0
        )
        lower_here = factor_panel(
            matrix_tile[:, offset : offset + width], diag_block, offset, first_row
        )
        rows_here = broadcast(lower_here, "col", 0)
        cols_here = broadcast(rows_here, "row", my_col // per_owner)
        matrix_tile = outer_update(matrix_tile, rows_here, cols_here)
        gathered_rows.append(rows_here)
    pair_all = jnp.concatenate(gathered_rows, 1)
    kept_row = global_row >= 2 * width
    kept_col = global_col >= 2 * width
    trailing = jnp.where(kept_row & kept_col, matrix_tile, 0.0)
    share = 2 * width // col_count
    panels = lax.dynamic_slice_in_dim(pair_all, my_col * share, share, 1)
    return (trailing, panels)


def solution(mesh):
    placed = (P("row", "col"), P())
    return jax.shard_map(
        body,
        mesh=mesh,
        in_specs=placed,
        out_specs=(P("row", "col"), P("row", "col")),
        check_vma=False,
    )
```

profile of v0, /device:TPU:2, one launch (start us, length us, event | category | flops | bytes accessed | tf_op | source)
XLA Modules:
  0.0 1477.9 jit_solution(5546559407506952772)
XLA Ops:
  7.2 1.2 dynamic_slice.6
  9.2 1.7 multiply_convert_fusion
  10.9 74.5 %all-gather.2.cloned.1.call-done = bf16[2048,800]{0,1:T(8,128)(2,1)} async-done(((bf16[128,800]{0,1:T(8,128)(2,1)}), bf16[2048,800]{0,1:T(8,128)(2,1)}) %all-gather.2.cloned.1.call-update) | async-done | bytes 3276816 | tf_op jit(solution)/shard_map/all_gather | solution.py:47
  85.4 2.0 broadcast_select_fusion
  87.5 178.2 %all-reduce.9.cloned.1.call-done = bf16[2048,800]{0,1:T(8,128)(2,1)} async-done(((bf16[2048,800]{0,1:T(8,128)(2,1)}), bf16[2048,800]{0,1:T(8,128)(2,1)}) %all-reduce.9.cloned.1.call-update) | async-done | bytes 3276816 | tf_op jit(solution)/shard_map/psum | solution.py:17
  265.7 6.6 multiply_select_fusion
  272.3 0.8 slice_select_fusion.1
  273.1 0.3 all-reduce.13.cloned.1.call-start
  273.4 1.0 slice_bitcast_fusion.1
  274.4 178.6 %all-reduce.11.cloned.1.call-done = f32[256,256]{0,1:T(8,128)} async-done(((f32[256,256]{0,1:T(8,128)}), f32[256,256]{0,1:T(8,128)}) %all-reduce.11.cloned.1.call-update) | async-done | bytes 262160 | tf_op jit(solution)/shard_map/psum | solution.py:17
  453.0 1.1 copy.6
  454.1 1.0 fusion.8
  455.1 11.7 cholesky.130
  466.9 9.8 custom-call.13
  476.7 0.2 constant_dynamic-update-slice_fusion.3
  476.9 0.3 convolution_subtract_fusion.4
  477.2 11.7 cholesky.147
  488.9 0.7 compare_reduce_fusion.2
  489.6 0.7 compare_reduce_fusion.3
  491.7 4.5 while.4
  492.2 0.6 fusion.39
  492.8 1.4 bitcast_dynamic-update-slice_fusion.4
  494.2 0.6 fusion.39
  494.8 1.4 bitcast_dynamic-update-slice_fusion.4
  496.2 19.7 %custom-call.14 = f32[2,128,128]{1,2,0:T(8,128)S(1)} custom-call(f32[2,128,128]{2,1,0:T(8,128)S(1)} %get-tuple-element.18), custom_call_target="InvertDiagBlocksLowerTriangular" | custom-call | tf_op jit(solution)/shard_map/jit(_solve_triangular)/triangular_solve | solution.py:23
  515.9 1.9 fusion.4
  517.8 1.6 convolution_subtract_fusion.2
  519.4 0.9 fusion.16
  520.4 1.0 fusion
  521.4 158.2 %all-reduce.13.cloned.1.call-done = f32[800,256]{1,0:T(8,128)} async-done(((f32[800,256]{1,0:T(8,128)}), f32[800,256]{1,0:T(8,128)}) %all-reduce.13.cloned.1.call-update) | async-done | bytes 819216 | tf_op jit(solution)/shard_map/psum | solution.py:17
  679.6 1.0 broadcast_select_fusion.2
  680.6 186.0 %all-reduce.15.cloned.1.call-done = f32[800,256]{1,0:T(8,128)} async-done(((f32[800,256]{1,0:T(8,128)}), f32[800,256]{1,0:T(8,128)}) %all-reduce.15.cloned.1.call-update) | async-done | bytes 819216 | tf_op jit(solution)/shard_map/psum | solution.py:17
  866.6 5.1 convolution_subtract_fusion
  871.7 0.7 slice_select_fusion
  872.5 0.2 all-reduce.19.cloned.1.call-start
  872.7 1.0 slice_bitcast_fusion
  873.7 171.6 %all-reduce.17.cloned.1.call-done = f32[256,256]{0,1:T(8,128)} async-done(((f32[256,256]{0,1:T(8,128)}), f32[256,256]{0,1:T(8,128)}) %all-reduce.17.cloned.1.call-update) | async-done | bytes 262160 | tf_op jit(solution)/shard_map/psum | solution.py:17
  1045.3 1.1 copy.8
  1046.4 1.0 fusion.7
  1047.4 11.7 cholesky.164
  1059.2 9.8 custom-call.15
  1069.0 0.2 constant_dynamic-update-slice_fusion.1
  1069.2 0.3 convolution_subtract_fusion.3
  1069.5 11.7 cholesky.181
  1081.3 0.7 compare_reduce_fusion
  1082.0 0.7 compare_reduce_fusion.1
  1084.0 4.2 while.5
  1084.2 0.6 fusion.40
  1084.8 1.3 bitcast_dynamic-update-slice_fusion.5
  1086.2 0.6 fusion.40
  1086.8 1.3 bitcast_dynamic-update-slice_fusion.5
  1088.2 0.6 copy-done.3
  1088.8 20.5 %custom-call.16 = f32[2,128,128]{1,2,0:T(8,128)S(1)} custom-call(f32[2,128,128]{2,1,0:T(8,128)} %copy-done.3), custom_call_target="InvertDiagBlocksLowerTriangular" | custom-call | tf_op jit(solution)/shard_map/jit(_solve_triangular)/triangular_solve | solution.py:23
  1109.3 1.9 fusion.2
  1111.2 1.6 convolution_subtract_fusion.1
  1112.8 0.9 fusion.12
  1113.8 1.0 fusion.1
  1114.9 158.2 %all-reduce.19.cloned.1.call-done = f32[800,256]{1,0:T(8,128)} async-done(((f32[800,256]{1,0:T(8,128)}), f32[800,256]{1,0:T(8,128)}) %all-reduce.19.cloned.1.call-update) | async-done | bytes 819216 | tf_op jit(solution)/shard_map/psum | solution.py:17
  1273.0 0.9 broadcast_select_fusion.1
  1274.0 1.3 fusion.6
  1275.3 0.8 copy.12
  1276.2 184.7 %all-reduce.21.cloned.1.call-done = f32[800,256]{1,0:T(8,128)} async-done(((f32[800,256]{1,0:T(8,128)}), f32[800,256]{1,0:T(8,128)}) %all-reduce.21.cloned.1.call-update) | async-done | bytes 819216 | tf_op jit(solution)/shard_map/psum | solution.py:17
  1460.9 5.9 subtract_select_fusion
  1466.7 4.1 copy.11
  (47 shorter events, 1.0 us)
Async XLA Ops:
  7.2 78.3 %all-gather.2.cloned.1.call-start = ((), (), s32[]{:S(2)}) async-start(), calls=%async_computation | async-start | bytes 3481600 | tf_op jit(solution)/shard_map/all_gather | solution.py:47
  10.8 254.9 %all-reduce.9.cloned.1.call-start = ((), (), s32[]{:S(2)}) async-start(), calls=%async_computation.1 | async-start | bytes 6553600 | tf_op jit(solution)/shard_map/psum | solution.py:17
  87.4 365.6 %all-reduce.11.cloned.1.call-start = ((), (), s32[]{:S(2)}) async-start(), calls=%async_computation.2 | async-start | bytes 524288 | tf_op jit(solution)/shard_map/psum | solution.py:17
  272.3 219.3 %copy-start = (f32[800,800]{0,1:T(8,128)}, f32[800,800]{0,1:T(8,128)S(1)}, u32[]{:S(2)}) copy-start(f32[800,800]{0,1:T(8,128)S(1)} %multiply_select_fusion) | copy-start | bytes 7680004
  273.1 406.5 %all-reduce.13.cloned.1.call-start = ((), (), s32[]{:S(2)}) async-start(), calls=%async_computation.3 | async-start | bytes 1638400 | tf_op jit(solution)/shard_map/psum | solution.py:17
  488.9 2.6 copy-start.1
  521.4 345.3 %all-reduce.15.cloned.1.call-start = ((), (), s32[]{:S(2)}) async-start(), calls=%async_computation.4 | async-start | bytes 1638400 | tf_op jit(solution)/shard_map/psum | solution.py:17
  680.6 364.7 %all-reduce.17.cloned.1.call-start = ((), (), s32[]{:S(2)}) async-start(), calls=%async_computation.5 | async-start | bytes 524288 | tf_op jit(solution)/shard_map/psum | solution.py:17
  872.5 400.5 %all-reduce.19.cloned.1.call-start = ((), (), s32[]{:S(2)}) async-start(), calls=%async_computation.6 | async-start | bytes 1638400 | tf_op jit(solution)/shard_map/psum | solution.py:17
  1081.2 2.6 copy-start.2
  1088.2 0.7 copy-start.3
  1114.8 346.1 %all-reduce.21.cloned.1.call-start = ((), (), s32[]{:S(2)}) async-start(), calls=%async_computation.7 | async-start | bytes 1638400 | tf_op jit(solution)/shard_map/psum | solution.py:17
Sparse Core Ops, SparseCore 0:
  11.1 74.2 all-gather.1
  88.1 177.5 all-reduce.8
  273.2 179.7 all-reduce.10
  521.5 158.0 all-reduce.12
  682.1 184.5 all-reduce.14
  872.6 172.6 all-reduce.16
  1114.9 158.0 all-reduce.18
  1276.4 184.3 all-reduce.20
where the time goes:
time: 1480 us
  waiting for transfers between devices  1290 us (87%)
  other arithmetic  122 us (8%)
  matrix products  27.2 us (2%)
  local copies, waits for them, and re-layouts  19.1 us (1%)
  between operations  17.9 us (1%)
    psum x7, waiting for transfers between devices, broadcast(): return lax.psum(jnp.where(mine, shard, jnp.zeros_like(shard)), axis)  1220 us
    all_gather x1, waiting for transfers between devices, body(): col_slab = lax.all_gather(scaled, 'row', axis=0, tiled=True)  74.5 us
    another operation x14, other arithmetic, factor_panel(): factor_lower = jnp.linalg.cholesky(diag_block)  69.3 us
    another operation x5, other arithmetic, factor_panel(): jax.scipy.linalg.solve_triangular(factor_lower, panel_strip.T, lower=True)  40.3 us
  transfers between devices with their start and end apart: 8, of which 8 were waited for; matrix products, arithmetic and copies ran while one was open for 0% of the time, Pallas kernels for 0%

commit v1 on v0

v1 whole, which is shorter than its diff:
```python
import jax
import jax.numpy as jnp
from jax import lax
from jax.experimental import pallas as pl
from jax.experimental.pallas import tpu as pltpu
from jax.sharding import PartitionSpec as P

TOK = 128
PANEL = 256
LEAF = 16

alpha_scale = 0.9
ridge_value = 0.2

F32 = jnp.float32
BF = jnp.bfloat16
MESH = pl.DeviceIdType.MESH


def dot_nt(a, b):
    return lax.dot_general(a, b, (((1,), (1,)), ((), ())), preferred_element_type=F32)


def dot_tn(a, b):
    return lax.dot_general(a, b, (((0,), (0,)), ((), ())), preferred_element_type=F32)


def split3(x):
    high = x.astype(BF)
    rest = x - high.astype(F32)
    mid = rest.astype(BF)
    low = (rest - mid.astype(F32)).astype(BF)
    return high, mid, low


def six_left(x):
    h, m, l = split3(x)
    return jnp.concatenate([h, h, h, m, m, l], 0)


def six_right(x):
    h, m, l = split3(x)
    return jnp.concatenate([h, m, l, h, m, h], 0)


def two(x):
    high = x.astype(BF)
    return high, (x - high.astype(F32)).astype(BF)


def sub_cast(x, s):
    return jnp.broadcast_to(x[s : s + 1, :], (8, 128))


def lane_cast(x, k):
    return jnp.broadcast_to(x[:, k : k + 1], (8, 128))


def chain8(s, rows, cols):
    for k in range(8):
        r = lax.rsqrt(s[k, k])
        for j in range(k + 1, 8):
            s[j, k] = s[j, k] * r
        for q in range(k + 1, 8):
            for j in range(q, 8):
                s[j, q] = s[j, q] - s[j, k] * s[q, k]
        rows[k] = rows[k] * r
        for j in range(k + 1, 8):
            rows[j] = rows[j] - s[j, k] * rows[k]
        if cols is not None:
            cols[k] = cols[k] * r
            for q in range(k + 1, 8):
                cols[q] = cols[q] - cols[k] * s[q, k]


def leaf_factor(m4, kb, leaf):
    i0 = kb * 16 + 2 * leaf
    o = LEAF * leaf
    d0 = m4[i0, kb]
    d1 = m4[i0 + 1, kb]
    s = {}
    for k in range(8):
        column = lane_cast(d0, o + k)
        for j in range(k, 8):
            s[j, k] = sub_cast(column, j)
    cols = [lane_cast(d1, o + k) for k in range(16)]
    upper = [m4[i0, :, q, :] for q in range(8)]
    first = cols[:8]
    chain8(s, upper, first)
    for q in range(8):
        m4[i0, :, q, :] = upper[q]
    lower = [m4[i0 + 1, :, q, :] for q in range(8)]
    second = cols[8:]
    for k in range(8):
        t = [sub_cast(first[k], q) for q in range(8)]
        for q in range(8):
            second[q] = second[q] - first[k] * t[q]
        for q in range(8):
            lower[q] = lower[q] - t[q] * upper[k]
    s = {}
    for k in range(8):
        for j in range(k, 8):
            s[j, k] = sub_cast(second[k], j)
    chain8(s, lower, None)
    for q in range(8):
        m4[i0 + 1, :, q, :] = lower[q]


def inner_update(m4, kb, leaf):
    i0 = kb * 16 + 2 * leaf
    u = m4[pl.ds(i0, 2), pl.ds(kb, 5)]
    tiles = [u[:, t].reshape(16, 128) for t in range(5)]
    left = six_left(tiles[0])[:, LEAF * (leaf + 1) :]
    up = dot_tn(left, six_right(jnp.concatenate(tiles, 1)))
    for q in range((7 - leaf) * 2):
        for t in range(5):
            m4[i0 + 2 + q, kb + t] = (
                m4[i0 + 2 + q, kb + t] - up[8 * q : 8 * q + 8, 128 * t : 128 * t + 128]
            )


def rest_update(m4, kb, b):
    left = six_left(m4[pl.ds(kb * 16, 16), b].reshape(128, 128))
    for half in range(2):
        w = jnp.concatenate(
            [m4[pl.ds(kb * 16, 16), kb + 1 + 2 * half + t].reshape(128, 128) for t in range(2)], 1
        )
        up = dot_tn(left, six_right(w))
        for t in range(2):
            tt = kb + 1 + 2 * half + t
            m4[pl.ds(b * 16, 16), tt] = m4[pl.ds(b * 16, 16), tt] - up[
                :, 128 * t : 128 * t + 128
            ].reshape(16, 8, 128)


def factor(m4):
    def block(kb, _):
        for leaf in range(8):
            leaf_factor(m4, kb, leaf)
            if leaf < 7:
                inner_update(m4, kb, leaf)

        def rest(b, _):
            rest_update(m4, kb, b)
            return 0

        lax.fori_loop(kb + 1, 4, rest, 0)
        return 0

    lax.fori_loop(0, 4, block, 0)


def gather_kernel(act, weight, cs, rs, ss, send, crecv, rrecv, srecv):
    r = lax.axis_index("row")
    c = lax.axis_index("col")
    y, h, k = r // 4, (r // 2) % 2, r % 2
    x, l = c // 4, c % 4

    def row_at(yy, hh, kk):
        return 4 * ((yy + 4) % 4) + 2 * hh + kk

    def col_at(xx, ll):
        return 4 * ((xx + 4) % 4) + ll

    zring = [(r, col_at(x, (l + d) % 4)) for d in (1, 2, 3)]
    zring += [(row_at(y, 1 - h, k), col_at(x, (l + d) % 4)) for d in (0, 1, 2, 3)]
    partners = zring + [
        (r, col_at(x + 1, l)),
        (r, col_at(x - 1, l)),
        (row_at(y + 1, h, k), c),
        (row_at(y - 1, h, k), c),
        (row_at(y, h, 1 - k), c),
    ]
    barrier = pltpu.get_barrier_semaphore()
    for p in partners:
        pl.semaphore_signal(barrier, inc=1, device_id=p, device_id_type=MESH)

    @pl.when(r != c)
    def _():
        pl.semaphore_signal(barrier, inc=1, device_id=(c, r), device_id_type=MESH)

    value = jnp.full((8, 128), weight[r], F32)
    scale = jnp.sqrt(value / TOK)[0:1, 0:1]
    for f in range(0, 800, 128):
        n = min(128, 800 - f)
        part = (act[:, f : f + n].astype(F32) * scale).astype(BF).astype(F32)
        cs[r, f : f + n, :] = part.T.astype(BF)

    pl.semaphore_wait(barrier, jnp.where(r == c, len(partners), len(partners) + 1))

    pending = []
    count = [0]

    def copy(src, dst, recv, target, cond=None):
        d = pltpu.make_async_remote_copy(
            src_ref=src,
            dst_ref=dst,
            send_sem=send.at[count[0]],
            recv_sem=recv,
            device_id=target,
            device_id_type=MESH,
        )
        count[0] += 1
        if cond is None:
            d.start()
        else:
            pl.when(cond)(d.start)
        pending.append((cond, d))

    def send_c(t, target):
        copy(cs.at[t], cs.at[t], crecv.at[t], target)

    def send_r(t, target):
        copy(rs.at[t], rs.at[t], rrecv.at[t], target)

    def s_ref(t, half):
        return ss.at[t, pl.ds(256 * half, 256)]

    def send_s(t, half, target, cond=None):
        copy(s_ref(t, half), s_ref(t, half), srecv.at[t, half], target, cond)

    def arrived(ref, sem):
        pltpu.make_async_remote_copy(
            src_ref=ref, dst_ref=ref, send_sem=send.at[0], recv_sem=sem, device_id=(r, c), device_id_type=MESH
        ).wait_recv()

    def wait_c(t):
        arrived(cs.at[t], crecv.at[t])

    def wait_r(t):
        arrived(rs.at[t], rrecv.at[t])

    def wait_s(t, half):
        arrived(s_ref(t, half), srecv.at[t, half])

    twin = row_at(y, 1 - h, k)
    up, down = row_at(y + 1, h, k), row_at(y - 1, h, k)
    right, left = col_at(x + 1, l), col_at(x - 1, l)
    other = row_at(y, h, 1 - k)

    @pl.when(c == 0)
    def _():
        ss[r] = cs[r, 0:512]

    at_l0 = l == 0
    source = c == 0
    side = jnp.logical_and(at_l0, x % 2 == 1)
    for half in range(2):
        send_s(r, half, (r, 4), source)
        send_s(r, half, (r, 12), source)

    @pl.when(r == c)
    def _():
        rs[c] = cs[r]

    copy(cs.at[r], rs.at[r], rrecv.at[r], (c, r), r != c)
    send_c(r, (twin, c))
    send_c(r, (up, c))
    send_c(r, (down, c))

    for half in range(2):

        @pl.when(jnp.logical_and(at_l0, x != 0))
        def _():
            wait_s(r, half)

        send_s(r, half, (r, 8), jnp.logical_and(at_l0, x == 1 + 2 * half))
        for p in zring:
            send_s(r, half, p, at_l0)

    for half in range(2):

        @pl.when(l != 0)
        def _():
            wait_s(r, half)

        wait_s(twin, half)
        for t in (r, twin):
            send_s(t, half, (up, c))
            send_s(t, half, (down, c))
            send_s(t, half, (other, c))

    for half in range(2):
        for hh in range(2):
            wait_s(row_at(y - 1, hh, k), half)
            wait_s(row_at(y + 1, hh, k), half)
        send_s(row_at(y - 1, 0, k), half, (up, c))
        send_s(row_at(y + 1, 1, k), half, (down, c))
        for hh in range(2):
            send_s(row_at(y - 1, hh, k), half, (other, c))
            send_s(row_at(y + 1, hh, k), half, (other, c))

    @pl.when(r != c)
    def _():
        wait_r(c)

    for d in (1, 2, 3):
        send_r(c, (r, col_at(x, (l + d) % 4)))
    send_r(c, (r, right))
    send_r(c, (r, left))

    wait_c(twin)
    send_c(twin, (up, c))
    send_c(twin, (down, c))
    send_c(r, (other, c))
    send_c(twin, (other, c))

    for half in range(2):
        for hh in range(2):
            wait_s(row_at(y + 2, hh, k), half)
            send_s(row_at(y + 2, hh, k), half, (other, c))

    for d in (1, 2, 3):
        t = col_at(x, (l + d) % 4)
        wait_r(t)
        send_r(t, (r, right))
        send_r(t, (r, left))

    for hh in range(2):
        wait_c(row_at(y - 1, hh, k))
        wait_c(row_at(y + 1, hh, k))
    send_c(row_at(y - 1, 0, k), (up, c))
    send_c(row_at(y + 1, 1, k), (down, c))
    for hh in range(2):
        send_c(row_at(y - 1, hh, k), (other, c))
        send_c(row_at(y + 1, hh, k), (other, c))

    for d in range(4):
        ll = (l + d) % 4
        wait_r(col_at(x - 1, ll))
        wait_r(col_at(x + 1, ll))
        if d < 2:
            send_r(col_at(x - 1, ll), (r, right))
        else:
            send_r(col_at(x + 1, ll), (r, left))

    for hh in range(2):
        wait_c(row_at(y + 2, hh, k))
        send_c(row_at(y + 2, hh, k), (other, c))
    for ll in range(4):
        wait_r(col_at(x + 2, ll))
    for d in range(4):
        for hh in range(2):
            wait_c(row_at(y + d, hh, 1 - k))
            for half in range(2):
                wait_s(row_at(y + d, hh, 1 - k), half)

    for cond, d in pending:
        if cond is None:
            d.wait_send()
        else:
            pl.when(cond)(d.wait_send)


def compute_kernel(cs, rs, ss, trailing, panels, m4, yr, yc, pr, pc):
    r = lax.axis_index("row")
    c = lax.axis_index("col")
    s_all = jnp.concatenate([ss[t] for t in range(16)], 1)
    for n in range(2):
        g = dot_nt(s_all, s_all[256 * n : 256 * n + 256])
        i = lax.broadcasted_iota(jnp.int32, (512, 256), 0)
        j = lax.broadcasted_iota(jnp.int32, (512, 256), 1) + 256 * n
        g = jnp.where(i == j, g + ridge_value, alpha_scale * g)
        for t in range(2):
            m4[:, 2 * n + t] = g[:, 128 * t : 128 * t + 128].reshape(64, 8, 128)
            m4[:, 4 + 2 * n + t] = jnp.where(i == j, 1.0, 0.0)[:, 128 * t : 128 * t + 128].reshape(64, 8, 128)
    factor(m4)

    c_all = jnp.concatenate([cs[t] for t in range(16)], 1)
    r_all = jnp.concatenate([rs[t] for t in range(16)], 1)
    for n in range(2):
        yr[:, 256 * n : 256 * n + 256] = alpha_scale * dot_nt(r_all, s_all[256 * n : 256 * n + 256])
        yc[:, 256 * n : 256 * n + 256] = alpha_scale * dot_nt(c_all, s_all[256 * n : 256 * n + 256])

    wide = [jnp.concatenate([m4[pl.ds(16 * b, 16), 4 + t].reshape(128, 128) for b in range(4)], 0) for t in range(4)]
    w_high, w_low = two(jnp.concatenate(wide, 1))
    for y_ref, p_ref in ((yr, pr), (yc, pc)):
        y_high, y_low = two(y_ref[...])
        p = dot_nt(
            jnp.concatenate([y_high, y_high, y_low], 1), jnp.concatenate([w_high, w_low, w_high], 1)
        )
        p_ref[...] = p

    w_mine = jnp.concatenate([m4[pl.ds(4 * c, 4), 4 + t].reshape(32, 128) for t in range(4)], 1)
    wm_high, wm_low = two(w_mine)
    y_high, y_low = two(yr[...])
    mine = dot_nt(
        jnp.concatenate([y_high, y_high, y_low], 1), jnp.concatenate([wm_high, wm_low, wm_high], 1)
    )
    panels[...] = mine
    u_row = lax.broadcasted_iota(jnp.int32, (128, 128), 0) + 32 * c

    @pl.when(r == 0)
    def _():
        for t in range(4):
            u = m4[pl.ds(4 * c, 4), t].reshape(32, 128)
            u = jnp.concatenate([u, u, u, u], 0)
            j = lax.broadcasted_iota(jnp.int32, (128, 128), 1) + 128 * t
            u = jnp.where(j >= u_row, u, 0.0)
            panels[128 * t : 128 * t + 128, :] = u.T[:, 0:32]

    pr_high, pr_low = two(pr[...])
    pc_high, pc_low = two(pc[...])
    p_left = jnp.concatenate([pr_high, pr_high, pr_low], 1)
    p_right = jnp.concatenate([pc_high, pc_low, pc_high], 1)
    row0 = jnp.where(r == 0, 512, 0)
    col0 = jnp.where(c == 0, 512, 0)
    for n in range(0, 800, 256):
        w = min(256, 800 - n)
        g = dot_nt(r_all, c_all[n : n + w])
        pp = dot_nt(p_left, p_right[n : n + w])
        i = lax.broadcasted_iota(jnp.int32, (800, w), 0)
        j = lax.broadcasted_iota(jnp.int32, (800, w), 1) + n
        m = jnp.where(i == jnp.where(r == c, j, -1), g + ridge_value, alpha_scale * g) - pp
        trailing[:, n : n + w] = jnp.where(jnp.logical_and(i >= row0, j >= col0), m, 0.0)


def body(activations, task_weight):
    vmem = pl.BlockSpec(memory_space=pltpu.VMEM)
    slab = jax.ShapeDtypeStruct((16, 800, 128), BF)
    first = jax.ShapeDtypeStruct((16, 512, 128), BF)
    cs, rs, ss = pl.pallas_call(
        gather_kernel,
        out_shape=(slab, slab, first),
        in_specs=[vmem, pl.BlockSpec(memory_space=pltpu.SMEM)],
        out_specs=(vmem, vmem, vmem),
        scratch_shapes=[
            pltpu.SemaphoreType.DMA((128,)),
            pltpu.SemaphoreType.DMA((16,)),
            pltpu.SemaphoreType.DMA((16,)),
            pltpu.SemaphoreType.DMA((16, 2)),
        ],
        compiler_params=pltpu.CompilerParams(
            collective_id=0, has_side_effects=True, vmem_limit_bytes=60 << 20
        ),
    )(activations, task_weight)
    return pl.pallas_call(
        compute_kernel,
        out_shape=(
            jax.ShapeDtypeStruct((800, 800), F32),
            jax.ShapeDtypeStruct((800, 32), F32),
        ),
        in_specs=[vmem] * 3,
        out_specs=(vmem, vmem),
        scratch_shapes=[
            pltpu.VMEM((64, 8, 8, 128), F32),
            pltpu.VMEM((800, 512), F32),
            pltpu.VMEM((800, 512), F32),
            pltpu.VMEM((800, 512), F32),
            pltpu.VMEM((800, 512), F32),
        ],
        compiler_params=pltpu.CompilerParams(vmem_limit_bytes=60 << 20),
    )(cs, rs, ss)


def solution(mesh):
    placed = (P("row", "col"), P())
    return jax.shard_map(
        body,
        mesh=mesh,
        in_specs=placed,
        out_specs=(P("row", "col"), P("row", "col")),
        check_vma=False,
    )
```

time: 1480 us -> 142 us (0.10)
  the two profiles are of different devices: /device:TPU:2 before, /device:TPU:32 now
where the time goes in v1:
time: 142 us
  Pallas kernels  137 us (96%)
  local copies, waits for them, and re-layouts  3.58 us (3%)
    pallas_call x1, Pallas kernels, body(): pl.pallas_call(gather_kernel, out_shape=(slab, slab, first), in_specs=[vm...  88 us
    pallas_call x1, Pallas kernels, body(): pl.pallas_call(compute_kernel, out_shape=(jax.ShapeDtypeStruct((800, 800)...  49.3 us

profile of v1, /device:TPU:32, one launch (start us, length us, event | category | flops | bytes accessed | tf_op | source)
XLA Modules:
  0.0 141.6 jit_solution(9694682285212523028)
XLA Ops:
  0.6 1.8 %copy.4.act = bf16[128,800]{1,0:T(8,128)(2,1)} copy(bf16[128,800]{0,1:T(8,128)(2,1)} %param.2) | data formatting | bytes 409600 | tf_op args[0]
  2.4 88.0 %shard_map.41 = (bf16[16,800,128]{2,1,0:T(8,128)(2,1)}, bf16[16,800,128]{2,1,0:T(8,128)(2,1)}, bf16[16,512,128]{2,1,0:T(8,128)(2,1)}) custom-call(bf16[128,800]{1,0:T(8,128)(2,1)} %copy.4.act, f32[16]{0:T(128)} %weight.1), custom_call_target="tpu_custom_call" | custom-call | tf_op jit(solution)/shard_map/pallas_call | solution.py:422
  90.4 49.3 %shard_map.42 = (f32[800,800]{1,0:T(8,128)}, f32[800,32]{1,0:T(8,128)}) custom-call(bf16[16,800,128]{2,1,0:T(8,128)(2,1)} %get-tuple-element.5.cs, bf16[16,800,128]{2,1,0:T(8,128)(2,1)} %get-tuple-element.6.rs, bf16[16,512,128]{2,1,0:T(8,128)(2,1)} %get-tuple-element.7.ss), custom_call_target="tpu_custom_call" | custom-call | tf_op jit(solution)/shard_map/pallas_call | solution.py:437
  139.8 1.8 %copy.5 = f32[800,32]{0,1:T(8,128)} copy(f32[800,32]{1,0:T(8,128)} %get-tuple-element.9) | data formatting | bytes 204800 | tf_op jit(solution)/shard_map/pallas_call | solution.py:437

commit v2 on v1

--- a/solution.py
+++ b/solution.py
@@ -133,9 +133,12 @@
             ].reshape(16, 8, 128)
 
 
-def factor(m4):
+def factor(m4, hooks):
     def block(kb, _):
         for leaf in range(8):
+            for at, run in hooks:
+                if at % 8 == leaf:
+                    pl.when(kb == at // 8)(run)
             leaf_factor(m4, kb, leaf)
             if leaf < 7:
                 inner_update(m4, kb, leaf)
@@ -150,7 +153,7 @@
     lax.fori_loop(0, 4, block, 0)
 
 
-def gather_kernel(act, weight, cs, rs, ss, send, crecv, rrecv, srecv):
+def kernel(act, weight, trailing, panels, cs, rs, ss, m4, yr, yc, pr, pc, send, crecv, rrecv, srecv):
     r = lax.axis_index("row")
     c = lax.axis_index("col")
     y, h, k = r // 4, (r // 2) % 2, r % 2
@@ -179,33 +182,35 @@
     def _():
         pl.semaphore_signal(barrier, inc=1, device_id=(c, r), device_id_type=MESH)
 
-    value = jnp.full((8, 128), weight[r], F32)
-    scale = jnp.sqrt(value / TOK)[0:1, 0:1]
-    for f in range(0, 800, 128):
-        n = min(128, 800 - f)
-        part = (act[:, f : f + n].astype(F32) * scale).astype(BF).astype(F32)
-        cs[r, f : f + n, :] = part.T.astype(BF)
+    scale = jnp.sqrt(jnp.full((8, 128), weight[r], F32) / TOK)[0:1, 0:1]
+    cs[r] = (act[...].astype(F32) * scale).astype(BF)
+
+    @pl.when(c == 0)
+    def _():
+        ss[r] = cs[r, 0:512]
+
+    @pl.when(r == c)
+    def _():
+        rs[c] = cs[r]
 
     pl.semaphore_wait(barrier, jnp.where(r == c, len(partners), len(partners) + 1))
 
     pending = []
-    count = [0]
 
     def copy(src, dst, recv, target, cond=None):
         d = pltpu.make_async_remote_copy(
             src_ref=src,
             dst_ref=dst,
-            send_sem=send.at[count[0]],
+            send_sem=send.at[len(pending)],
             recv_sem=recv,
             device_id=target,
             device_id_type=MESH,
         )
-        count[0] += 1
         if cond is None:
             d.start()
         else:
             pl.when(cond)(d.start)
-        pending.append((cond, d))
+        pending.append((cond, src))
 
     def send_c(t, target):
         copy(cs.at[t], cs.at[t], crecv.at[t], target)
@@ -238,25 +243,12 @@
     right, left = col_at(x + 1, l), col_at(x - 1, l)
     other = row_at(y, h, 1 - k)
 
-    @pl.when(c == 0)
-    def _():
-        ss[r] = cs[r, 0:512]
-
     at_l0 = l == 0
     source = c == 0
-    side = jnp.logical_and(at_l0, x % 2 == 1)
     for half in range(2):
         send_s(r, half, (r, 4), source)
         send_s(r, half, (r, 12), source)
-
-    @pl.when(r == c)
-    def _():
-        rs[c] = cs[r]
-
     copy(cs.at[r], rs.at[r], rrecv.at[r], (c, r), r != c)
-    send_c(r, (twin, c))
-    send_c(r, (up, c))
-    send_c(r, (down, c))
 
     for half in range(2):
 
@@ -280,6 +272,15 @@
             send_s(t, half, (down, c))
             send_s(t, half, (other, c))
 
+    @pl.when(r != c)
+    def _():
+        wait_r(c)
+
+    for d in (1, 2, 3):
+        send_r(c, (r, col_at(x, (l + d) % 4)))
+    send_r(c, (r, right))
+    send_r(c, (r, left))
+
     for half in range(2):
         for hh in range(2):
             wait_s(row_at(y - 1, hh, k), half)
@@ -290,114 +291,126 @@
             send_s(row_at(y - 1, hh, k), half, (other, c))
             send_s(row_at(y + 1, hh, k), half, (other, c))
 
-    @pl.when(r != c)
-    def _():
-        wait_r(c)
-
-    for d in (1, 2, 3):
-        send_r(c, (r, col_at(x, (l + d) % 4)))
-    send_r(c, (r, right))
-    send_r(c, (r, left))
-
-    wait_c(twin)
-    send_c(twin, (up, c))
-    send_c(twin, (down, c))
+    send_c(r, (twin, c))
+    send_c(r, (up, c))
+    send_c(r, (down, c))
     send_c(r, (other, c))
-    send_c(twin, (other, c))
 
     for half in range(2):
         for hh in range(2):
             wait_s(row_at(y + 2, hh, k), half)
             send_s(row_at(y + 2, hh, k), half, (other, c))
-
-    for d in (1, 2, 3):
-        t = col_at(x, (l + d) % 4)
+    for d in range(4):
+        for hh in range(2):
+            for half in range(2):
+                wait_s(row_at(y + d, hh, 1 - k), half)
+
+    near = [col_at(x, (l + d) % 4) for d in range(4)]
+    on_left = [col_at(x - 1, (l + d) % 4) for d in range(4)]
+    on_right = [col_at(x + 1, (l + d) % 4) for d in range(4)]
+    below = [row_at(y - 1, hh, k) for hh in range(2)]
+    above = [row_at(y + 1, hh, k) for hh in range(2)]
+    beyond = [row_at(y + 2, hh, k) for hh in range(2)]
+
+    def line(d):
+        t = near[d]
         wait_r(t)
         send_r(t, (r, right))
         send_r(t, (r, left))
 
-    for hh in range(2):
-        wait_c(row_at(y - 1, hh, k))
-        wait_c(row_at(y + 1, hh, k))
-    send_c(row_at(y - 1, 0, k), (up, c))
-    send_c(row_at(y + 1, 1, k), (down, c))
-    for hh in range(2):
-        send_c(row_at(y - 1, hh, k), (other, c))
-        send_c(row_at(y + 1, hh, k), (other, c))
-
-    for d in range(4):
-        ll = (l + d) % 4
-        wait_r(col_at(x - 1, ll))
-        wait_r(col_at(x + 1, ll))
+    def ring(d):
+        wait_r(on_left[d])
+        wait_r(on_right[d])
         if d < 2:
-            send_r(col_at(x - 1, ll), (r, right))
+            send_r(on_left[d], (r, right))
         else:
-            send_r(col_at(x + 1, ll), (r, left))
-
-    for hh in range(2):
-        wait_c(row_at(y + 2, hh, k))
-        send_c(row_at(y + 2, hh, k), (other, c))
-    for ll in range(4):
-        wait_r(col_at(x + 2, ll))
-    for d in range(4):
-        for hh in range(2):
-            wait_c(row_at(y + d, hh, 1 - k))
-            for half in range(2):
-                wait_s(row_at(y + d, hh, 1 - k), half)
-
-    for cond, d in pending:
-        if cond is None:
-            d.wait_send()
-        else:
-            pl.when(cond)(d.wait_send)
-
-
-def compute_kernel(cs, rs, ss, trailing, panels, m4, yr, yc, pr, pc):
-    r = lax.axis_index("row")
-    c = lax.axis_index("col")
+            send_r(on_right[d], (r, left))
+
+    def twins():
+        wait_c(twin)
+        send_c(twin, (up, c))
+        send_c(twin, (down, c))
+        send_c(twin, (other, c))
+
+    def ends():
+        for hh in range(2):
+            wait_c(below[hh])
+            wait_c(above[hh])
+        send_c(below[0], (up, c))
+        send_c(above[1], (down, c))
+        for hh in range(2):
+            send_c(below[hh], (other, c))
+            send_c(above[hh], (other, c))
+
+    def far():
+        for hh in range(2):
+            wait_c(beyond[hh])
+            send_c(beyond[hh], (other, c))
+
+    hooks = [
+        (3, lambda: line(1)),
+        (6, lambda: line(2)),
+        (8, lambda: ring(0)),
+        (10, twins),
+        (11, lambda: line(3)),
+        (14, lambda: ring(1)),
+        (17, ends),
+        (20, lambda: ring(2)),
+        (23, lambda: ring(3)),
+        (25, far),
+    ]
+
     s_all = jnp.concatenate([ss[t] for t in range(16)], 1)
     for n in range(2):
         g = dot_nt(s_all, s_all[256 * n : 256 * n + 256])
         i = lax.broadcasted_iota(jnp.int32, (512, 256), 0)
         j = lax.broadcasted_iota(jnp.int32, (512, 256), 1) + 256 * n
         g = jnp.where(i == j, g + ridge_value, alpha_scale * g)
+        one = jnp.where(i == j, 1.0, 0.0)
         for t in range(2):
             m4[:, 2 * n + t] = g[:, 128 * t : 128 * t + 128].reshape(64, 8, 128)
-            m4[:, 4 + 2 * n + t] = jnp.where(i == j, 1.0, 0.0)[:, 128 * t : 128 * t + 128].reshape(64, 8, 128)
-    factor(m4)
-
+            m4[:, 4 + 2 * n + t] = one[:, 128 * t : 128 * t + 128].reshape(64, 8, 128)
+    factor(m4, hooks)
+
+    for d in range(4):
+        for hh in range(2):
+            wait_c(row_at(y + d, hh, 1 - k))
+    s_again = jnp.concatenate([ss[t] for t in range(16)], 1)
     c_all = jnp.concatenate([cs[t] for t in range(16)], 1)
+    for n in range(2):
+        yc[:, 256 * n : 256 * n + 256] = alpha_scale * dot_nt(c_all, s_again[256 * n : 256 * n + 256])
+
+    wide = [jnp.concatenate([m4[pl.ds(16 * b, 16), 4 + t].reshape(128, 128) for b in range(4)], 0) for t in range(4)]
+    w_high, w_low = two(jnp.concatenate(wide, 1))
+    w_right = jnp.concatenate([w_high, w_low, w_high], 1)
+
+    def solve(y_ref, p_ref):
+        y_high, y_low = two(y_ref[...])
+        p_ref[...] = dot_nt(jnp.concatenate([y_high, y_high, y_low], 1), w_right)
+
+    solve(yc, pc)
+
+    for ll in range(4):
+        wait_r(col_at(x + 2, ll))
     r_all = jnp.concatenate([rs[t] for t in range(16)], 1)
     for n in range(2):
-        yr[:, 256 * n : 256 * n + 256] = alpha_scale * dot_nt(r_all, s_all[256 * n : 256 * n + 256])
-        yc[:, 256 * n : 256 * n + 256] = alpha_scale * dot_nt(c_all, s_all[256 * n : 256 * n + 256])
-
-    wide = [jnp.concatenate([m4[pl.ds(16 * b, 16), 4 + t].reshape(128, 128) for b in range(4)], 0) for t in range(4)]
-    w_high, w_low = two(jnp.concatenate(wide, 1))
-    for y_ref, p_ref in ((yr, pr), (yc, pc)):
-        y_high, y_low = two(y_ref[...])
-        p = dot_nt(
-            jnp.concatenate([y_high, y_high, y_low], 1), jnp.concatenate([w_high, w_low, w_high], 1)
-        )
-        p_ref[...] = p
+        yr[:, 256 * n : 256 * n + 256] = alpha_scale * dot_nt(r_all, s_again[256 * n : 256 * n + 256])
+    solve(yr, pr)
 
     w_mine = jnp.concatenate([m4[pl.ds(4 * c, 4), 4 + t].reshape(32, 128) for t in range(4)], 1)
     wm_high, wm_low = two(w_mine)
     y_high, y_low = two(yr[...])
-    mine = dot_nt(
-        jnp.concatenate([y_high, y_high, y_low], 1), jnp.concatenate([wm_high, wm_low, wm_high], 1)
+    panels[...] = dot_nt(
+        jnp.concatenate([wm_high, wm_low, wm_high], 1), jnp.concatenate([y_high, y_high, y_low], 1)
     )
-    panels[...] = mine
-    u_row = lax.broadcasted_iota(jnp.int32, (128, 128), 0) + 32 * c
 
     @pl.when(r == 0)
     def _():
+        i = lax.broadcasted_iota(jnp.int32, (32, 128), 0) + 32 * c
         for t in range(4):
             u = m4[pl.ds(4 * c, 4), t].reshape(32, 128)
-            u = jnp.concatenate([u, u, u, u], 0)
-            j = lax.broadcasted_iota(jnp.int32, (128, 128), 1) + 128 * t
-            u = jnp.where(j >= u_row, u, 0.0)
-            panels[128 * t : 128 * t + 128, :] = u.T[:, 0:32]
+            j = lax.broadcasted_iota(jnp.int32, (32, 128), 1) + 128 * t
+            panels[:, 128 * t : 128 * t + 128] = jnp.where(j >= i, u, 0.0)
 
     pr_high, pr_low = two(pr[...])
     pc_high, pc_low = two(pc[...])
@@ -414,18 +427,36 @@
         m = jnp.where(i == jnp.where(r == c, j, -1), g + ridge_value, alpha_scale * g) - pp
         trailing[:, n : n + w] = jnp.where(jnp.logical_and(i >= row0, j >= col0), m, 0.0)
 
+    for at, (cond, src) in enumerate(pending):
+        sent = pltpu.make_async_remote_copy(
+            src_ref=src, dst_ref=src, send_sem=send.at[at], recv_sem=crecv.at[0], device_id=(other, c), device_id_type=MESH
+        ).wait_send
+        if cond is None:
+            sent()
+        else:
+            pl.when(cond)(sent)
+
 
 def body(activations, task_weight):
     vmem = pl.BlockSpec(memory_space=pltpu.VMEM)
-    slab = jax.ShapeDtypeStruct((16, 800, 128), BF)
-    first = jax.ShapeDtypeStruct((16, 512, 128), BF)
-    cs, rs, ss = pl.pallas_call(
-        gather_kernel,
-        out_shape=(slab, slab, first),
+    trailing, panels = pl.pallas_call(
+        kernel,
+        out_shape=(
+            jax.ShapeDtypeStruct((800, 800), F32),
+            jax.ShapeDtypeStruct((32, 800), F32),
+        ),
         in_specs=[vmem, pl.BlockSpec(memory_space=pltpu.SMEM)],
-        out_specs=(vmem, vmem, vmem),
+        out_specs=(vmem, vmem),
         scratch_shapes=[
-            pltpu.SemaphoreType.DMA((128,)),
+            pltpu.VMEM((16, 800, 128), BF),
+            pltpu.VMEM((16, 800, 128), BF),
+            pltpu.VMEM((16, 512, 128), BF),
+            pltpu.VMEM((64, 8, 8, 128), F32),
+            pltpu.VMEM((800, 512), F32),
+            pltpu.VMEM((800, 512), F32),
+            pltpu.VMEM((800, 512), F32),
+            pltpu.VMEM((800, 512), F32),
+            pltpu.SemaphoreType.DMA((96,)),
             pltpu.SemaphoreType.DMA((16,)),
             pltpu.SemaphoreType.DMA((16,)),
             pltpu.SemaphoreType.DMA((16, 2)),
@@ -433,24 +464,8 @@
         compiler_params=pltpu.CompilerParams(
             collective_id=0, has_side_effects=True, vmem_limit_bytes=60 << 20
         ),
-    )(activations, task_weight)
-    return pl.pallas_call(
-        compute_kernel,
-        out_shape=(
-            jax.ShapeDtypeStruct((800, 800), F32),
-            jax.ShapeDtypeStruct((800, 32), F32),
-        ),
-        in_specs=[vmem] * 3,
-        out_specs=(vmem, vmem),
-        scratch_shapes=[
-            pltpu.VMEM((64, 8, 8, 128), F32),
-            pltpu.VMEM((800, 512), F32),
-            pltpu.VMEM((800, 512), F32),
-            pltpu.VMEM((800, 512), F32),
-            pltpu.VMEM((800, 512), F32),
-        ],
-        compiler_params=pltpu.CompilerParams(vmem_limit_bytes=60 << 20),
-    )(cs, rs, ss)
+    )(activations.T, task_weight)
+    return trailing, panels.T
 
 
 def solution(mesh):

time: 142 us -> 106 us (0.75)
  the two profiles are of different devices: /device:TPU:32 before, /device:TPU:40 now
where the time goes in v2:
time: 106 us
  Pallas kernels  101 us (95%)
  local copies, waits for them, and re-layouts  4.25 us (4%)
    pallas_call x1, Pallas kernels, body(): pl.pallas_call(kernel, out_shape=(jax.ShapeDtypeStruct((800, 800), F32),...  101 us
    unnamed x4, local copies, waits for them, and re-layouts  4.25 us

profile of v2, /device:TPU:40, one launch (start us, length us, event | category | flops | bytes accessed | tf_op | source)
XLA Modules:
  0.0 105.7 jit_solution(10141881079987039566)
XLA Ops:
  0.6 100.8 %shard_map.41 = (f32[800,800]{1,0:T(8,128)}, f32[32,800]{1,0:T(8,128)}) custom-call(bf16[800,128]{1,0:T(8,128)(2,1)} %bitcast.2, f32[16]{0:T(128)} %weight.1), custom_call_target="tpu_custom_call" | custom-call | tf_op jit(solution)/shard_map/pallas_call | solution.py:442
  101.4 0.0 copy-start
  101.4 3.6 %copy.6 = f32[800,800]{1,0:T(8,128)} copy(f32[800,800]{1,0:T(8,128)} %get-tuple-element.8) | data formatting | bytes 5120000
  105.0 0.0 copy-done
  105.0 0.6 copy.7
Async XLA Ops:
  101.4 3.6 %copy-start = (f32[32,800]{1,0:T(8,128)S(1)}, f32[32,800]{1,0:T(8,128)}, u32[]{:S(2)}) copy-start(f32[32,800]{1,0:T(8,128)} %get-tuple-element.5) | copy-start | bytes 307204

commit v3 on v2

--- a/solution.py
+++ b/solution.py
@@ -8,6 +8,7 @@
 TOK = 128
 PANEL = 256
 LEAF = 16
+PIECES = ((0, 128), (128, 128), (256, 256))
 
 alpha_scale = 0.9
 ridge_value = 0.2
@@ -147,7 +148,7 @@
             rest_update(m4, kb, b)
             return 0
 
-        lax.fori_loop(kb + 1, 4, rest, 0)
+        lax.fori_loop(kb + 1, jnp.where(kb < 2, kb + 1, 4), rest, 0)
         return 0
 
     lax.fori_loop(0, 4, block, 0)
@@ -163,7 +164,16 @@
         return 4 * ((yy + 4) % 4) + 2 * hh + kk
 
     def col_at(xx, ll):
-        return 4 * ((xx + 4) % 4) + ll
+        return 4 * ((xx + 8) % 4) + ll
+
+    def slot_at(xx, ll):
+        return 4 * ((2 * y - xx + 8) % 4) + 2 * ((ll // 2 + k + h) % 2) + ll % 2
+
+    mine = slot_at(x, l)
+    goes_row = c
+    goes_col = col_at(2 * x - y, 2 * ((h + l // 2 + l % 2) % 2) + k)
+    moves = jnp.logical_or(goes_row != r, goes_col != c)
+    stays = jnp.logical_not(moves)
 
     zring = [(r, col_at(x, (l + d) % 4)) for d in (1, 2, 3)]
     zring += [(row_at(y, 1 - h, k), col_at(x, (l + d) % 4)) for d in (0, 1, 2, 3)]
@@ -173,14 +183,16 @@
         (row_at(y + 1, h, k), c),
         (row_at(y - 1, h, k), c),
         (row_at(y, h, 1 - k), c),
+        (r, col_at(x + 2, l)),
+        (row_at(y + 2, h, k), c),
     ]
     barrier = pltpu.get_barrier_semaphore()
     for p in partners:
         pl.semaphore_signal(barrier, inc=1, device_id=p, device_id_type=MESH)
 
-    @pl.when(r != c)
+    @pl.when(moves)
     def _():
-        pl.semaphore_signal(barrier, inc=1, device_id=(c, r), device_id_type=MESH)
+        pl.semaphore_signal(barrier, inc=1, device_id=(mine, r), device_id_type=MESH)
 
     scale = jnp.sqrt(jnp.full((8, 128), weight[r], F32) / TOK)[0:1, 0:1]
     cs[r] = (act[...].astype(F32) * scale).astype(BF)
@@ -189,11 +201,11 @@
     def _():
         ss[r] = cs[r, 0:512]
 
-    @pl.when(r == c)
+    @pl.when(stays)
     def _():
-        rs[c] = cs[r]
-
-    pl.semaphore_wait(barrier, jnp.where(r == c, len(partners), len(partners) + 1))
+        rs[r] = cs[r]
+
+    pl.semaphore_wait(barrier, jnp.where(stays, len(partners), len(partners) + 1))
 
     pending = []
 
@@ -219,7 +231,7 @@
         copy(rs.at[t], rs.at[t], rrecv.at[t], target)
 
     def s_ref(t, half):
-        return ss.at[t, pl.ds(256 * half, 256)]
+        return ss.at[t, pl.ds(*PIECES[half])]
 
     def send_s(t, half, target, cond=None):
         copy(s_ref(t, half), s_ref(t, half), srecv.at[t, half], target, cond)
@@ -243,96 +255,116 @@
     right, left = col_at(x + 1, l), col_at(x - 1, l)
     other = row_at(y, h, 1 - k)
 
-    at_l0 = l == 0
-    source = c == 0
-    for half in range(2):
-        send_s(r, half, (r, 4), source)
-        send_s(r, half, (r, 12), source)
-    copy(cs.at[r], rs.at[r], rrecv.at[r], (c, r), r != c)
-
-    for half in range(2):
-
-        @pl.when(jnp.logical_and(at_l0, x != 0))
-        def _():
-            wait_s(r, half)
-
-        send_s(r, half, (r, 8), jnp.logical_and(at_l0, x == 1 + 2 * half))
-        for p in zring:
-            send_s(r, half, p, at_l0)
-
-    for half in range(2):
-
-        @pl.when(l != 0)
-        def _():
-            wait_s(r, half)
-
-        wait_s(twin, half)
-        for t in (r, twin):
-            send_s(t, half, (up, c))
-            send_s(t, half, (down, c))
-            send_s(t, half, (other, c))
-
-    @pl.when(r != c)
-    def _():
-        wait_r(c)
-
-    for d in (1, 2, 3):
-        send_r(c, (r, col_at(x, (l + d) % 4)))
-    send_r(c, (r, right))
-    send_r(c, (r, left))
-
-    for half in range(2):
-        for hh in range(2):
-            wait_s(row_at(y - 1, hh, k), half)
-            wait_s(row_at(y + 1, hh, k), half)
-        send_s(row_at(y - 1, 0, k), half, (up, c))
-        send_s(row_at(y + 1, 1, k), half, (down, c))
-        for hh in range(2):
-            send_s(row_at(y - 1, hh, k), half, (other, c))
-            send_s(row_at(y + 1, hh, k), half, (other, c))
-
-    send_c(r, (twin, c))
-    send_c(r, (up, c))
-    send_c(r, (down, c))
-    send_c(r, (other, c))
-
-    for half in range(2):
-        for hh in range(2):
-            wait_s(row_at(y + 2, hh, k), half)
-            send_s(row_at(y + 2, hh, k), half, (other, c))
-    for d in range(4):
-        for hh in range(2):
-            for half in range(2):
-                wait_s(row_at(y + d, hh, 1 - k), half)
-
-    near = [col_at(x, (l + d) % 4) for d in range(4)]
-    on_left = [col_at(x - 1, (l + d) % 4) for d in range(4)]
-    on_right = [col_at(x + 1, (l + d) % 4) for d in range(4)]
+    down_line = [jnp.maximum(l - d, 0) for d in range(4)]
+    up_line = [jnp.minimum(l + d, 3) for d in range(4)]
+    minus = [slot_at(x, ll) for ll in down_line]
+    plus = [slot_at(x, ll) for ll in up_line]
+    minus_on_left = [slot_at(x - 1, ll) for ll in down_line]
+    minus_on_right = [slot_at(x + 1, ll) for ll in down_line]
+    plus_on_left = [slot_at(x - 1, ll) for ll in up_line]
+    plus_on_right = [slot_at(x + 1, ll) for ll in up_line]
+    from_minus = [l >= d for d in range(4)]
+    from_plus = [l + d <= 3 for d in range(4)]
+    pass_plus = [jnp.logical_and(l >= d, l <= 2) for d in range(4)]
+    pass_minus = [jnp.logical_and(l + d <= 3, l >= 1) for d in range(4)]
+    odd_slot = [(c + d) % 2 == 1 for d in range(4)]
+    even_slot = [(c + d) % 2 == 0 for d in range(4)]
+    side = [
+        [jnp.logical_and(v, p) for v, p in zip(f, par)]
+        for f in (from_minus, from_plus)
+        for par in (even_slot, odd_slot)
+    ]
+    before, after = 4 * x + down_line[1], 4 * x + up_line[1]
     below = [row_at(y - 1, hh, k) for hh in range(2)]
     above = [row_at(y + 1, hh, k) for hh in range(2)]
     beyond = [row_at(y + 2, hh, k) for hh in range(2)]
-
-    def line(d):
-        t = near[d]
-        wait_r(t)
-        send_r(t, (r, right))
-        send_r(t, (r, left))
-
-    def ring(d):
-        wait_r(on_left[d])
-        wait_r(on_right[d])
-        if d < 2:
-            send_r(on_left[d], (r, right))
-        else:
-            send_r(on_right[d], (r, left))
-
-    def twins():
+    across = [row_at(y + d, hh, 1 - k) for d in range(4) for hh in range(2)]
+    own_two = (r, twin)
+    far_row, far_col = row_at(y + 2, h, k), col_at(x + 2, l)
+
+    at_l0 = l == 0
+    off_l0 = l != 0
+    source = c == 0
+    passes_z = jnp.logical_and(at_l0, x != 0)
+
+    def s_x(half):
+        for target in (right, left, far_col):
+            send_s(r, half, (r, target), source)
+
+    def s_z(half):
+        pl.when(passes_z)(lambda: wait_s(r, half))
+        for p in zring:
+            send_s(r, half, p, at_l0)
+
+    def s_y(half):
+        pl.when(off_l0)(lambda: wait_s(r, half))
+        wait_s(twin, half)
+        for t in own_two:
+            send_s(t, half, (up, c))
+            send_s(t, half, (down, c))
+            send_s(t, half, (far_row, c))
+        for t in own_two:
+            send_s(t, half, (other, c))
+
+    def s_core(half):
+        for group in (below, above, beyond):
+            for t in group:
+                wait_s(t, half)
+                send_s(t, half, (other, c))
+
+    def s_end(half):
+        for t in across:
+            wait_s(t, half)
+
+    def r_first():
+        pl.when(moves)(lambda: wait_r(mine))
+        copy(rs.at[mine], rs.at[mine], rrecv.at[mine], (r, after), pass_plus[0])
+        copy(rs.at[mine], rs.at[mine], rrecv.at[mine], (r, before), pass_minus[0])
+        send_r(mine, (r, right))
+        send_r(mine, (r, left))
+
+    def r_line(d):
+        def from_before():
+            wait_r(minus[d])
+
+        def from_after():
+            wait_r(plus[d])
+
+        pl.when(from_minus[d])(from_before)
+        pl.when(from_plus[d])(from_after)
+        copy(rs.at[minus[d]], rs.at[minus[d]], rrecv.at[minus[d]], (r, after), pass_plus[d])
+        copy(rs.at[plus[d]], rs.at[plus[d]], rrecv.at[plus[d]], (r, before), pass_minus[d])
+        for target in (right, left):
+            copy(rs.at[minus[d]], rs.at[minus[d]], rrecv.at[minus[d]], (r, target), from_minus[d])
+            copy(rs.at[plus[d]], rs.at[plus[d]], rrecv.at[plus[d]], (r, target), from_plus[d])
+
+    def r_ring(d):
+        ways = [(from_minus, minus_on_left, minus_on_right, 0)]
+        if d > 0:
+            ways.append((from_plus, plus_on_left, plus_on_right, 2))
+        for there, on_left, on_right, at in ways:
+
+            def both():
+                wait_r(on_left[d])
+                wait_r(on_right[d])
+
+            pl.when(there[d])(both)
+            copy(rs.at[on_left[d]], rs.at[on_left[d]], rrecv.at[on_left[d]], (r, right), side[at][d])
+            copy(rs.at[on_right[d]], rs.at[on_right[d]], rrecv.at[on_right[d]], (r, left), side[at + 1][d])
+
+    def c_first():
+        send_c(r, (twin, c))
+        send_c(r, (up, c))
+        send_c(r, (down, c))
+        send_c(r, (other, c))
+
+    def c_twin():
         wait_c(twin)
         send_c(twin, (up, c))
         send_c(twin, (down, c))
         send_c(twin, (other, c))
 
-    def ends():
+    def c_pass():
         for hh in range(2):
             wait_c(below[hh])
             wait_c(above[hh])
@@ -342,34 +374,76 @@
             send_c(below[hh], (other, c))
             send_c(above[hh], (other, c))
 
-    def far():
+    def c_far():
         for hh in range(2):
             wait_c(beyond[hh])
             send_c(beyond[hh], (other, c))
 
+    def bring(piece):
+        base, wide = PIECES[piece]
+        p, w = base // 128, wide // 128
+        s_old = jnp.concatenate([ss[t, 0:base] for t in range(16)], 1)
+        s_new = jnp.concatenate([ss[t, base : base + wide] for t in range(16)], 1)
+        g_new = dot_nt(s_new, s_new)
+        i = lax.broadcasted_iota(jnp.int32, (wide, wide), 0)
+        j = lax.broadcasted_iota(jnp.int32, (wide, wide), 1)
+        m_new = jnp.where(i == j, g_new + ridge_value, alpha_scale * g_new)
+        one = jnp.where(i == j, 1.0, 0.0)
+        if base:
+            g_mix = alpha_scale * dot_nt(s_old, s_new)
+            w_old = jnp.concatenate([m4[0 : 16 * p, 4 + t].reshape(base, 128) for t in range(p)], 1)
+            wh, wm, wl = split3(w_old)
+            u = jnp.dot(
+                jnp.concatenate([wh, wh, wh, wm, wm, wl], 1), six_right(g_mix), preferred_element_type=F32
+            )
+            below_it = dot_tn(six_left(u), six_right(jnp.concatenate([u, w_old], 1)))
+            m_new = m_new - below_it[:, :wide]
+        rows = slice(16 * p, 16 * (p + w))
+        for t in range(w):
+            cut = slice(128 * t, 128 * t + 128)
+            if base:
+                m4[0 : 16 * p, p + t] = u[:, cut].reshape(16 * p, 8, 128)
+            m4[rows, p + t] = m_new[:, cut].reshape(16 * w, 8, 128)
+            m4[rows, 4 + p + t] = one[:, cut].reshape(16 * w, 8, 128)
+        for t in range(p):
+            m4[rows, 4 + t] = (-below_it[:, wide + 128 * t : wide + 128 * t + 128]).reshape(16 * w, 8, 128)
+
+    s_x(0)
+    copy(cs.at[r], rs.at[r], rrecv.at[r], (goes_row, goes_col), moves)
+    s_x(1)
+    s_x(2)
+    s_z(0)
+    s_z(1)
+    s_z(2)
+    s_y(0)
+    r_first()
+    s_core(0)
+    s_y(1)
+    s_end(0)
+
     hooks = [
-        (3, lambda: line(1)),
-        (6, lambda: line(2)),
-        (8, lambda: ring(0)),
-        (10, twins),
-        (11, lambda: line(3)),
-        (14, lambda: ring(1)),
-        (17, ends),
-        (20, lambda: ring(2)),
-        (23, lambda: ring(3)),
-        (25, far),
+        (0, lambda: bring(0)),
+        (0, lambda: s_y(2)),
+        (1, c_first),
+        (2, lambda: r_line(1)),
+        (3, lambda: s_core(1)),
+        (5, lambda: r_ring(0)),
+        (6, lambda: r_line(2)),
+        (7, lambda: s_core(2)),
+        (8, lambda: s_end(1)),
+        (8, lambda: bring(1)),
+        (9, lambda: r_ring(1)),
+        (11, lambda: r_line(3)),
+        (13, c_twin),
+        (15, lambda: r_ring(2)),
+        (16, lambda: s_end(2)),
+        (16, lambda: bring(2)),
+        (19, c_pass),
+        (20, lambda: r_ring(3)),
+        (25, c_far),
     ]
 
-    s_all = jnp.concatenate([ss[t] for t in range(16)], 1)
-    for n in range(2):
-        g = dot_nt(s_all, s_all[256 * n : 256 * n + 256])
-        i = lax.broadcasted_iota(jnp.int32, (512, 256), 0)
-        j = lax.broadcasted_iota(jnp.int32, (512, 256), 1) + 256 * n
-        g = jnp.where(i == j, g + ridge_value, alpha_scale * g)
-        one = jnp.where(i == j, 1.0, 0.0)
-        for t in range(2):
-            m4[:, 2 * n + t] = g[:, 128 * t : 128 * t + 128].reshape(64, 8, 128)
-            m4[:, 4 + 2 * n + t] = one[:, 128 * t : 128 * t + 128].reshape(64, 8, 128)
+    m4[...] = jnp.zeros_like(m4)
     factor(m4, hooks)
 
     for d in range(4):
@@ -391,7 +465,7 @@
     solve(yc, pc)
 
     for ll in range(4):
-        wait_r(col_at(x + 2, ll))
+        wait_r(slot_at(x + 2, ll))
     r_all = jnp.concatenate([rs[t] for t in range(16)], 1)
     for n in range(2):
         yr[:, 256 * n : 256 * n + 256] = alpha_scale * dot_nt(r_all, s_again[256 * n : 256 * n + 256])
@@ -456,10 +530,10 @@
             pltpu.VMEM((800, 512), F32),
             pltpu.VMEM((800, 512), F32),
             pltpu.VMEM((800, 512), F32),
-            pltpu.SemaphoreType.DMA((96,)),
+            pltpu.SemaphoreType.DMA((128,)),
             pltpu.SemaphoreType.DMA((16,)),
             pltpu.SemaphoreType.DMA((16,)),
-            pltpu.SemaphoreType.DMA((16, 2)),
+            pltpu.SemaphoreType.DMA((16, 3)),
         ],
         compiler_params=pltpu.CompilerParams(
             collective_id=0, has_side_effects=True, vmem_limit_bytes=60 << 20

time: 106 us -> 93.1 us (0.88)
  the two profiles are of different devices: /device:TPU:40 before, /device:TPU:2 now
where the time goes in v3:
time: 93.1 us; the launch traced here: 92.9 us
  Pallas kernels  88 us (95%)
  local copies, waits for them, and re-layouts  4.25 us (5%)
    pallas_call x1, Pallas kernels, body(): pl.pallas_call(kernel, out_shape=(jax.ShapeDtypeStruct((800, 800), F32),...  88 us
    unnamed x4, local copies, waits for them, and re-layouts  4.25 us

profile of v3, /device:TPU:2, one launch (start us, length us, event | category | flops | bytes accessed | tf_op | source)
XLA Modules:
  0.0 92.9 jit_solution(3689433996800777259)
XLA Ops:
  0.6 88.0 %shard_map.41 = (f32[800,800]{1,0:T(8,128)}, f32[32,800]{1,0:T(8,128)}) custom-call(bf16[800,128]{1,0:T(8,128)(2,1)} %bitcast.2, f32[16]{0:T(128)} %weight.1), custom_call_target="tpu_custom_call" | custom-call | tf_op jit(solution)/shard_map/pallas_call | solution.py:516
  88.7 0.0 copy-start
  88.7 3.6 %copy.6 = f32[800,800]{1,0:T(8,128)} copy(f32[800,800]{1,0:T(8,128)} %get-tuple-element.8) | data formatting | bytes 5120000
  92.3 0.0 copy-done
  92.3 0.6 copy.7
Async XLA Ops:
  88.7 3.6 %copy-start = (f32[32,800]{1,0:T(8,128)S(1)}, f32[32,800]{1,0:T(8,128)}, u32[]{:S(2)}) copy-start(f32[32,800]{1,0:T(8,128)} %get-tuple-element.5) | copy-start | bytes 307204

commit v4 on v3

--- a/solution.py
+++ b/solution.py
@@ -134,24 +134,31 @@
             ].reshape(16, 8, 128)
 
 
-def factor(m4, hooks):
-    def block(kb, _):
+def factor(m4, hooks, beside):
+    def early(kb, _):
         for leaf in range(8):
             for at, run in hooks:
-                if at % 8 == leaf:
+                if at < 16 and at % 8 == leaf:
                     pl.when(kb == at // 8)(run)
             leaf_factor(m4, kb, leaf)
             if leaf < 7:
                 inner_update(m4, kb, leaf)
-
-        def rest(b, _):
-            rest_update(m4, kb, b)
-            return 0
-
-        lax.fori_loop(kb + 1, jnp.where(kb < 2, kb + 1, 4), rest, 0)
         return 0
 
-    lax.fori_loop(0, 4, block, 0)
+    lax.fori_loop(0, 2, early, 0)
+    for kb in (2, 3):
+        for leaf in range(8):
+            for at, run in hooks:
+                if at == 8 * kb + leaf:
+                    run()
+            for at, run in beside:
+                if at == 8 * kb + leaf:
+                    run()
+            leaf_factor(m4, kb, leaf)
+            if leaf < 7:
+                inner_update(m4, kb, leaf)
+        if kb == 2:
+            rest_update(m4, 2, 3)
 
 
 def kernel(act, weight, trailing, panels, cs, rs, ss, m4, yr, yc, pr, pc, send, crecv, rrecv, srecv):
@@ -280,6 +287,7 @@
     beyond = [row_at(y + 2, hh, k) for hh in range(2)]
     across = [row_at(y + d, hh, 1 - k) for d in range(4) for hh in range(2)]
     own_two = (r, twin)
+    opposite = [slot_at(x + 2, ll) for ll in range(4)]
     far_row, far_col = row_at(y + 2, h, k), col_at(x + 2, l)
 
     at_l0 = l == 0
@@ -378,6 +386,14 @@
         for hh in range(2):
             wait_c(beyond[hh])
             send_c(beyond[hh], (other, c))
+
+    def c_across(d):
+        for t in across[2 * d : 2 * d + 2]:
+            wait_c(t)
+
+    def r_end():
+        for t in opposite:
+            wait_r(t)
 
     def bring(piece):
         base, wide = PIECES[piece]
@@ -440,40 +456,61 @@
         (16, lambda: bring(2)),
         (19, c_pass),
         (20, lambda: r_ring(3)),
+        (17, lambda: c_across(0)),
+        (22, lambda: c_across(1)),
+        (23, lambda: c_across(3)),
         (25, c_far),
+        (28, lambda: c_across(2)),
+        (30, r_end),
     ]
 
     m4[...] = jnp.zeros_like(m4)
-    factor(m4, hooks)
-
-    for d in range(4):
-        for hh in range(2):
-            wait_c(row_at(y + d, hh, 1 - k))
-    s_again = jnp.concatenate([ss[t] for t in range(16)], 1)
-    c_all = jnp.concatenate([cs[t] for t in range(16)], 1)
-    for n in range(2):
-        yc[:, 256 * n : 256 * n + 256] = alpha_scale * dot_nt(c_all, s_again[256 * n : 256 * n + 256])
+
+    def group(slab, total, task_row, start):
+        tasks = [4 * task_row + q for q in range(4)]
+        add = dot_nt(
+            jnp.concatenate([slab[t] for t in tasks], 1), jnp.concatenate([ss[t] for t in tasks], 1)
+        )
+        total[...] = add if start else total[...] + add
+
+    group_own, group_left, group_right, group_far = [(2 * y - xx + 8) % 4 for xx in (x, x - 1, x + 1, x + 2)]
+    y_down, y_up, y_far = (y + 3) % 4, (y + 1) % 4, (y + 2) % 4
+    beside = [
+        (17, lambda: group(rs, yr, group_own, True)),
+        (18, lambda: group(cs, yc, y, True)),
+        (21, lambda: group(rs, yr, group_left, False)),
+        (22, lambda: group(rs, yr, group_right, False)),
+        (23, lambda: group(cs, yc, y_down, False)),
+        (24, lambda: group(cs, yc, y_up, False)),
+        (29, lambda: group(cs, yc, y_far, False)),
+        (31, lambda: group(rs, yr, group_far, False)),
+    ]
+    factor(m4, hooks, beside)
 
     wide = [jnp.concatenate([m4[pl.ds(16 * b, 16), 4 + t].reshape(128, 128) for b in range(4)], 0) for t in range(4)]
     w_high, w_low = two(jnp.concatenate(wide, 1))
-    w_right = jnp.concatenate([w_high, w_low, w_high], 1)
-
-    def solve(y_ref, p_ref):
-        y_high, y_low = two(y_ref[...])
-        p_ref[...] = dot_nt(jnp.concatenate([y_high, y_high, y_low], 1), w_right)
-
-    solve(yc, pc)
-
-    for ll in range(4):
-        wait_r(slot_at(x + 2, ll))
+
+    def solve(y_ref):
+        y_high, y_low = two(alpha_scale * y_ref[...])
+        parts = []
+        for n in (256, 512):
+            yh, yl = y_high[:, :n], y_low[:, :n]
+            wh, wl = w_high[n - 256 : n, :n], w_low[n - 256 : n, :n]
+            parts.append(
+                two(dot_nt(jnp.concatenate([yh, yh, yl], 1), jnp.concatenate([wh, wl, wh], 1)))
+            )
+        return [jnp.concatenate([p[q] for p in parts], 1) for q in range(2)]
+
+    pc_high, pc_low = solve(yc)
+    pc[...] = jnp.concatenate([pc_high, pc_low, pc_high], 1)
+    pr_high, pr_low = solve(yr)
+    pr[...] = jnp.concatenate([pr_high, pr_high, pr_low], 1)
+    c_all = jnp.concatenate([cs[t] for t in range(16)], 1)
     r_all = jnp.concatenate([rs[t] for t in range(16)], 1)
-    for n in range(2):
-        yr[:, 256 * n : 256 * n + 256] = alpha_scale * dot_nt(r_all, s_again[256 * n : 256 * n + 256])
-    solve(yr, pr)
 
     w_mine = jnp.concatenate([m4[pl.ds(4 * c, 4), 4 + t].reshape(32, 128) for t in range(4)], 1)
     wm_high, wm_low = two(w_mine)
-    y_high, y_low = two(yr[...])
+    y_high, y_low = two(alpha_scale * yr[...])
     panels[...] = dot_nt(
         jnp.concatenate([wm_high, wm_low, wm_high], 1), jnp.concatenate([y_high, y_high, y_low], 1)
     )
@@ -486,10 +523,7 @@
             j = lax.broadcasted_iota(jnp.int32, (32, 128), 1) + 128 * t
             panels[:, 128 * t : 128 * t + 128] = jnp.where(j >= i, u, 0.0)
 
-    pr_high, pr_low = two(pr[...])
-    pc_high, pc_low = two(pc[...])
-    p_left = jnp.concatenate([pr_high, pr_high, pr_low], 1)
-    p_right = jnp.concatenate([pc_high, pc_low, pc_high], 1)
+    p_left, p_right = pr[...], pc[...]
     row0 = jnp.where(r == 0, 512, 0)
     col0 = jnp.where(c == 0, 512, 0)
     for n in range(0, 800, 256):
@@ -528,8 +562,8 @@
             pltpu.VMEM((64, 8, 8, 128), F32),
             pltpu.VMEM((800, 512), F32),
             pltpu.VMEM((800, 512), F32),
-            pltpu.VMEM((800, 512), F32),
-            pltpu.VMEM((800, 512), F32),
+            pltpu.VMEM((800, 1536), BF),
+            pltpu.VMEM((800, 1536), BF),
             pltpu.SemaphoreType.DMA((128,)),
             pltpu.SemaphoreType.DMA((16,)),
             pltpu.SemaphoreType.DMA((16,)),

time: 93.1 us -> 86.9 us (0.933)
  Pallas kernels: 88 us -> 81.9 us
    pallas_call x1, Pallas kernels: 88 us -> 81.9 us  [body(): pl.pallas_call(kernel, out_shape=(jax.ShapeDtypeStruct((800, 800), F32),...]
where the time goes in v4:
time: 86.9 us; the launch traced here: 86.8 us
  Pallas kernels  81.9 us (94%)
  local copies, waits for them, and re-layouts  4.25 us (5%)
    pallas_call x1, Pallas kernels, body(): pl.pallas_call(kernel, out_shape=(jax.ShapeDtypeStruct((800, 800), F32),...  81.9 us
    unnamed x4, local copies, waits for them, and re-layouts  4.25 us

profile of v4, /device:TPU:2, one launch (start us, length us, event | category | flops | bytes accessed | tf_op | source)
XLA Modules:
  0.0 86.8 jit_solution(6321925188882138847)
XLA Ops:
  0.6 81.9 %shard_map.41 = (f32[800,800]{1,0:T(8,128)}, f32[32,800]{1,0:T(8,128)}) custom-call(bf16[800,128]{1,0:T(8,128)(2,1)} %bitcast.2, f32[16]{0:T(128)} %weight.1), custom_call_target="tpu_custom_call" | custom-call | tf_op jit(solution)/shard_map/pallas_call | solution.py:550
  82.5 0.0 copy-start
  82.5 3.6 %copy.6 = f32[800,800]{1,0:T(8,128)} copy(f32[800,800]{1,0:T(8,128)} %get-tuple-element.8) | data formatting | bytes 5120000
  86.1 0.0 copy-done
  86.1 0.6 copy.7
Async XLA Ops:
  82.5 3.6 %copy-start = (f32[32,800]{1,0:T(8,128)S(1)}, f32[32,800]{1,0:T(8,128)}, u32[]{:S(2)}) copy-start(f32[32,800]{1,0:T(8,128)} %get-tuple-element.5) | copy-start | bytes 307204

commit v5 on v4

--- a/solution.py
+++ b/solution.py
@@ -444,14 +444,14 @@
         (2, lambda: r_line(1)),
         (3, lambda: s_core(1)),
         (5, lambda: r_ring(0)),
-        (6, lambda: r_line(2)),
+        (7, lambda: r_line(2)),
         (7, lambda: s_core(2)),
         (8, lambda: s_end(1)),
         (8, lambda: bring(1)),
-        (9, lambda: r_ring(1)),
-        (11, lambda: r_line(3)),
+        (10, lambda: r_ring(1)),
+        (12, lambda: r_line(3)),
         (13, c_twin),
-        (15, lambda: r_ring(2)),
+        (16, lambda: r_ring(2)),
         (16, lambda: s_end(2)),
         (16, lambda: bring(2)),
         (19, c_pass),
@@ -459,7 +459,7 @@
         (17, lambda: c_across(0)),
         (22, lambda: c_across(1)),
         (23, lambda: c_across(3)),
-        (25, c_far),
+        (26, c_far),
         (28, lambda: c_across(2)),
         (30, r_end),
     ]

time: 86.9 us -> 85.8 us (0.987)
  Pallas kernels: 81.9 us -> 80.3 us
    pallas_call x1, Pallas kernels: 81.9 us -> 80.3 us  [body(): pl.pallas_call(kernel, out_shape=(jax.ShapeDtypeStruct((800, 800), F32),...]
where the time goes in v5:
time: 85.8 us; the launch traced here: 85.2 us
  Pallas kernels  80.3 us (94%)
  local copies, waits for them, and re-layouts  4.25 us (5%)
    pallas_call x1, Pallas kernels, body(): pl.pallas_call(kernel, out_shape=(jax.ShapeDtypeStruct((800, 800), F32),...  80.3 us
    unnamed x4, local copies, waits for them, and re-layouts  4.25 us

profile of v5, /device:TPU:2, one launch (start us, length us, event | category | flops | bytes accessed | tf_op | source)
XLA Modules:
  0.0 85.2 jit_solution(11548556643485658788)
XLA Ops:
  0.6 80.3 %shard_map.41 = (f32[800,800]{1,0:T(8,128)}, f32[32,800]{1,0:T(8,128)}) custom-call(bf16[800,128]{1,0:T(8,128)(2,1)} %bitcast.2, f32[16]{0:T(128)} %weight.1), custom_call_target="tpu_custom_call" | custom-call | tf_op jit(solution)/shard_map/pallas_call | solution.py:550
  80.9 0.0 copy-start
  81.0 3.6 %copy.6 = f32[800,800]{1,0:T(8,128)} copy(f32[800,800]{1,0:T(8,128)} %get-tuple-element.8) | data formatting | bytes 5120000
  84.6 0.0 copy-done
  84.6 0.6 copy.7
Async XLA Ops:
  80.9 3.6 %copy-start = (f32[32,800]{1,0:T(8,128)S(1)}, f32[32,800]{1,0:T(8,128)}, u32[]{:S(2)}) copy-start(f32[32,800]{1,0:T(8,128)} %get-tuple-element.5) | copy-start | bytes 307204

commit v6 on v5

--- a/solution.py
+++ b/solution.py
@@ -441,20 +441,20 @@
         (0, lambda: bring(0)),
         (0, lambda: s_y(2)),
         (1, c_first),
-        (2, lambda: r_line(1)),
+        (3, lambda: r_line(1)),
         (3, lambda: s_core(1)),
-        (5, lambda: r_ring(0)),
-        (7, lambda: r_line(2)),
+        (6, lambda: r_ring(0)),
+        (8, lambda: r_line(2)),
         (7, lambda: s_core(2)),
         (8, lambda: s_end(1)),
         (8, lambda: bring(1)),
-        (10, lambda: r_ring(1)),
-        (12, lambda: r_line(3)),
-        (13, c_twin),
-        (16, lambda: r_ring(2)),
+        (11, lambda: r_ring(1)),
+        (13, lambda: r_line(3)),
+        (14, c_twin),
+        (17, lambda: r_ring(2)),
         (16, lambda: s_end(2)),
         (16, lambda: bring(2)),
-        (19, c_pass),
+        (20, c_pass),
         (20, lambda: r_ring(3)),
         (17, lambda: c_across(0)),
         (22, lambda: c_across(1)),
@@ -475,6 +475,15 @@
 
     group_own, group_left, group_right, group_far = [(2 * y - xx + 8) % 4 for xx in (x, x - 1, x + 1, x + 2)]
     y_down, y_up, y_far = (y + 3) % 4, (y + 1) % 4, (y + 2) % 4
+    def early_columns():
+        first_w = jnp.concatenate([m4[0:32, 4 + t].reshape(256, 128) for t in range(2)], 1)
+        wh, wl = two(first_w)
+        yh, yl = two(alpha_scale * yc[:, 0:256])
+        high, low = two(dot_nt(jnp.concatenate([yh, yh, yl], 1), jnp.concatenate([wh, wl, wh], 1)))
+        pc[:, 0:256] = high
+        pc[:, 512:768] = low
+        pc[:, 1024:1280] = high
+
     beside = [
         (17, lambda: group(rs, yr, group_own, True)),
         (18, lambda: group(cs, yc, y, True)),
@@ -483,6 +492,7 @@
         (23, lambda: group(cs, yc, y_down, False)),
         (24, lambda: group(cs, yc, y_up, False)),
         (29, lambda: group(cs, yc, y_far, False)),
+        (30, early_columns),
         (31, lambda: group(rs, yr, group_far, False)),
     ]
     factor(m4, hooks, beside)
@@ -490,10 +500,10 @@
     wide = [jnp.concatenate([m4[pl.ds(16 * b, 16), 4 + t].reshape(128, 128) for b in range(4)], 0) for t in range(4)]
     w_high, w_low = two(jnp.concatenate(wide, 1))
 
-    def solve(y_ref):
+    def solve(y_ref, widths):
         y_high, y_low = two(alpha_scale * y_ref[...])
         parts = []
-        for n in (256, 512):
+        for n in widths:
             yh, yl = y_high[:, :n], y_low[:, :n]
             wh, wl = w_high[n - 256 : n, :n], w_low[n - 256 : n, :n]
             parts.append(
@@ -501,9 +511,11 @@
             )
         return [jnp.concatenate([p[q] for p in parts], 1) for q in range(2)]
 
-    pc_high, pc_low = solve(yc)
-    pc[...] = jnp.concatenate([pc_high, pc_low, pc_high], 1)
-    pr_high, pr_low = solve(yr)
+    pc_high, pc_low = solve(yc, (512,))
+    pc[:, 256:512] = pc_high
+    pc[:, 768:1024] = pc_low
+    pc[:, 1280:1536] = pc_high
+    pr_high, pr_low = solve(yr, (256, 512))
     pr[...] = jnp.concatenate([pr_high, pr_high, pr_low], 1)
     c_all = jnp.concatenate([cs[t] for t in range(16)], 1)
     r_all = jnp.concatenate([rs[t] for t in range(16)], 1)

time: 85.8 us -> 85.8 us (level)
  no operation moved by 1% of the time
where the time goes in v6:
time: 85.8 us; the launch traced here: 85.1 us
  Pallas kernels  80.2 us (93%)
  local copies, waits for them, and re-layouts  4.25 us (5%)
    pallas_call x1, Pallas kernels, body(): pl.pallas_call(kernel, out_shape=(jax.ShapeDtypeStruct((800, 800), F32),...  80.2 us
    unnamed x4, local copies, waits for them, and re-layouts  4.25 us

profile of v6, /device:TPU:2, one launch (start us, length us, event | category | flops | bytes accessed | tf_op | source)
XLA Modules:
  0.0 85.1 jit_solution(593488225607786761)
XLA Ops:
  0.6 80.2 %shard_map.41 = (f32[800,800]{1,0:T(8,128)}, f32[32,800]{1,0:T(8,128)}) custom-call(bf16[800,128]{1,0:T(8,128)(2,1)} %bitcast.2, f32[16]{0:T(128)} %weight.1), custom_call_target="tpu_custom_call" | custom-call | tf_op jit(solution)/shard_map/pallas_call | solution.py:562
  80.9 0.0 copy-start
  80.9 3.6 %copy.6 = f32[800,800]{1,0:T(8,128)} copy(f32[800,800]{1,0:T(8,128)} %get-tuple-element.8) | data formatting | bytes 5120000
  84.5 0.0 copy-done
  84.5 0.6 copy.7
Async XLA Ops:
  80.9 3.6 %copy-start = (f32[32,800]{1,0:T(8,128)S(1)}, f32[32,800]{1,0:T(8,128)}, u32[]{:S(2)}) copy-start(f32[32,800]{1,0:T(8,128)} %get-tuple-element.5) | copy-start | bytes 307204
